TPU v7x, 32 devices: a whole 2x2x4 slice. The times are simulated.
32 devices in a mesh: sector: 8 (over y, x, core), op: 4 (over z).
Axes of the slice: x: 2, y: 2, z: 4, core: 2. Of those that a mesh axis runs over, the one named last changes fastest.
Arguments:
- wave: bfloat16 [512, 768], P('sector'), may hold values from -6 to 6
- left_blocks: bfloat16 [24, 512, 64], P('op', 'sector'), may hold values from -0.75 to 0.75
- right_ops: bfloat16 [24, 768, 768], P('op'), may hold values from -0.21875 to 0.21875
- delta: int32 [24], P('op'), may hold values from -1 to 1
- active: int32 [24, 8], P('op', 'sector'), may hold values 0 or 1
- sector_rows: int32 [8], P('sector'), may hold values from 16 to 64
Outputs:
- sigma: bfloat16 [512, 768], P('sector', 'op')
All inputs are finite; a program needn't handle non-finite values. No bound on the sum of `active` on one device may be relied on, other than what follows from the above.
Results may differ from a plain program's by a relative error of at most 0.011.
Values sent between devices are 32-bit elements; how exact they have to be, the bound alone decides.
A program may use at most 64 MiB of HBM per device.

v0:
```python
import jax
import jax.numpy as jnp
from jax import lax
from jax.sharding import PartitionSpec as P


def passed_along(block, axis, distance):
    devices = range(lax.axis_size(axis))
    route = [(i - distance, i) for i in devices if i - distance in devices]
    return lax.ppermute(block, axis, route)


def on_device(wave, left_blocks, right_ops, delta, active, sector_rows):
    rows = jnp.arange(wave.shape[0], dtype=jnp.int32)
    live = rows < sector_rows[0]
    masked = jnp.where(live[:, None], wave, jnp.zeros_like(wave))
    inter = jnp.einsum("kij,jc->kic", left_blocks, masked, preferred_element_type=jnp.float32)
    inter = inter.astype(jnp.bfloat16)
    terms = jnp.einsum("kic,kcd->kid", inter, right_ops, preferred_element_type=jnp.float32)
    picks = (jnp.arange(3, dtype=jnp.int32)[:, None] == delta[None, :] + 1).astype(jnp.float32)
    weights = picks * active[:, 0].astype(jnp.float32)[None, :]
    parts = jnp.einsum("gk,kic->gic", weights, terms)
    shares = lax.psum_scatter(parts, "op", scatter_dimension=2, tiled=True)
    from_below = passed_along(shares[2], "sector", 1)
    from_above = passed_along(shares[0], "sector", -1)
    total = shares[1] + from_below + from_above
    total = jnp.where(live[:, None], total, 0.0)
    return total.astype(jnp.bfloat16)


def solution(mesh):
    return jax.shard_map(
        on_device,
        mesh=mesh,
        in_specs=(
            P("sector", None),
            P("op", "sector", None),
            P("op", None, None),
            P("op"),
            P("op", "sector"),
            P("sector"),
        ),
        out_specs=P("sector", "op"),
        check_vma=False,
    )
```

profile of v0, /device:TPU:1, one launch (start us, length us, event | category | flops | bytes accessed | tf_op | source)
XLA Modules:
  0.0 129.7 jit_solution(7425834390961494630)
XLA Ops:
  6.5 0.0 copy-start
  6.5 0.0 reduce-scatter.4.cloned.1.call-start
  7.2 0.7 broadcast_add_fusion
  7.9 0.7 convert_bitcast_fusion
  8.6 0.0 copy-done
  8.6 4.6 %fusion.3 = bf16[6,64,768]{2,1,0:T(8,128)(2,1)S(1)} fusion(bf16[6,768,768]{2,1,0:T(8,128)(2,1)} %param.8, bf16[6,64,64]{2,1,0:T(8,128)(2,1)S(1)} %copy-done, bf16[64,768]{1,0:T(8,128)(2,1)} %param.6, pred[64]{0:T(512)(128)(4,1)S(1)} %iota_compare_fusion.2), kind=kOutput, calls=%fused_computation.4 | convolution fusion | flops 491077632 | bytes 7815232 | tf_op jit(solution)/shard_map/kic,kcd->kid/dot_general | solution.py:19
  13.2 0.5 fusion
  13.7 20.0 %copy.14 = f32[3,64,768]{0,1,2:T(8,128)} copy(f32[3,64,768]{2,0,1:T(4,128)S(1)} %fusion) | data formatting | bytes 1179648
  33.6 19.1 %reshape.14 = f32[768,192]{1,0:T(8,128)} reshape(f32[768,64,3]{2,1,0:T(8,128)} %bitcast.30) | data formatting | bytes 1179648
  52.7 0.0 reduce-scatter.4.cloned.1.call-update
  52.7 24.3 %reduce-scatter.4.cloned.1.call-done = f32[192,192]{1,0:T(8,128)} async-done(((f32[768,192]{1,0:T(8,128)}), f32[192,192]{1,0:T(8,128)}) %reduce-scatter.4.cloned.1.call-update) | async-done | bytes 147472
  77.0 8.5 %reshape.15 = f32[192,64,3]{2,1,0:T(8,128)} reshape(f32[192,192]{1,0:T(8,128)} %reduce-scatter.4.cloned.1.call-done) | data formatting | bytes 294912
  85.5 14.8 %fusion.23 = (f32[1,64,192]{0,1,2:T(8,128)}, f32[1,64,192]{0,1,2:T(8,128)}, f32[1,64,192]{0,1,2:T(8,128)}) fusion(f32[3,64,192]{0,1,2:T(8,128)} %bitcast.31), kind=kLoop, calls=%fused_computation.24 | loop fusion | bytes 294912 | tf_op jit(solution)/shard_map/slice | solution.py:26
  100.3 5.0 %copy.17 = f32[1,64,192]{2,1,0:T(8,128)S(1)} copy(f32[1,64,192]{0,1,2:T(8,128)} %get-tuple-element.6) | data formatting | bytes 98304
  105.3 5.0 %copy.20 = f32[1,64,192]{2,1,0:T(8,128)S(1)} copy(f32[1,64,192]{0,1,2:T(8,128)} %get-tuple-element.7) | data formatting | bytes 98304
  110.3 4.9 %collective-permute-start = (f32[64,192]{1,0:T(8,128)S(1)}, f32[64,192]{1,0:T(8,128)S(1)}, u32[]{:S(2)}, u32[]{:S(2)}) collective-permute-start(f32[64,192]{1,0:T(8,128)S(1)} %bitcast.33), channel_id=1, source_target_pairs={{0,4},{4,8},{8,12},{12,16},{16,20},{20,24},{24,28},{1,5},{5,9},{9,... | collective-permute-start | bytes 147464 | tf_op jit(solution)/shard_map/ppermute | solution.py:10
  115.2 1.9 %collective-permute-start.1 = (f32[64,192]{1,0:T(8,128)S(1)}, f32[64,192]{1,0:T(8,128)S(1)}, u32[]{:S(2)}, u32[]{:S(2)}) collective-permute-start(f32[64,192]{1,0:T(8,128)S(1)} %bitcast.32), channel_id=1, source_target_pairs={{4,0},{8,4},{12,8},{16,12},{20,16},{24,20},{28,24},{5,1},{9,5},{13... | collective-permute-start | bytes 147464 | tf_op jit(solution)/shard_map/ppermute | solution.py:10
  117.1 5.0 %copy.19 = f32[1,64,192]{2,1,0:T(8,128)S(1)} copy(f32[1,64,192]{0,1,2:T(8,128)} %get-tuple-element.5) | data formatting | bytes 98304
  122.1 0.0 collective-permute-done
  122.1 0.0 collective-permute-done.1
  122.1 0.7 fusion.12
  (1 shorter events, 0.0 us)
Async XLA Ops:
  6.5 2.0 %copy-start = (bf16[6,64,64]{2,1,0:T(8,128)(2,1)S(1)}, bf16[6,64,64]{2,1,0:T(8,128)(2,1)}, u32[]{:S(2)}) copy-start(bf16[6,64,64]{2,1,0:T(8,128)(2,1)} %param.7) | copy-start | bytes 147460
  6.5 70.5 %reduce-scatter.4.cloned.1.call-start = ((), (), s32[]{:S(2)}) async-start(), calls=%async_computation.1 | async-start | bytes 983040
  110.3 11.9 %collective-permute-start = (f32[64,192]{1,0:T(8,128)S(1)}, f32[64,192]{1,0:T(8,128)S(1)}, u32[]{:S(2)}, u32[]{:S(2)}) collective-permute-start(f32[64,192]{1,0:T(8,128)S(1)} %bitcast.33), channel_id=1, source_target_pairs={{0,4},{4,8},{8,12},{12,16},{16,20},{20,24},{24,28},{1,5},{5,9},{9,... | collective-permute-start | bytes 147464 | tf_op jit(solution)/shard_map/ppermute | solution.py:10
  115.2 6.9 %collective-permute-start.1 = (f32[64,192]{1,0:T(8,128)S(1)}, f32[64,192]{1,0:T(8,128)S(1)}, u32[]{:S(2)}, u32[]{:S(2)}) collective-permute-start(f32[64,192]{1,0:T(8,128)S(1)} %bitcast.32), channel_id=1, source_target_pairs={{4,0},{8,4},{12,8},{16,12},{20,16},{24,20},{28,24},{5,1},{9,5},{13... | collective-permute-start | bytes 147464 | tf_op jit(solution)/shard_map/ppermute | solution.py:10
Sparse Core Ops, SparseCore 0:
  52.9 24.0 reduce-scatter.3
where the time goes:
time: 130 us
  local copies, waits for them, and re-layouts  77.3 us (59%)
  waiting for transfers between devices  24.3 us (19%)
  between operations  14.1 us (11%)
  starting transfers between devices  6.85 us (5%)
  matrix products  5.12 us (4%)
  other arithmetic  2.02 us (2%)
    unnamed x8, local copies, waits for them, and re-layouts  62.5 us
    unnamed x2, waiting for transfers between devices  24.3 us
    slice x1, local copies, waits for them, and re-layouts, on_device(): total = shares[1] + from_below + from_above  14.8 us
    ppermute x2, starting transfers between devices, passed_along(): return lax.ppermute(block, axis, route)  6.85 us
    dot_general x1, matrix products, on_device(): jnp.einsum('kic,kcd->kid', inter, right_ops, preferred_element_type=jnp.f...  4.64 us
  transfers between devices with their start and end apart: 3, of which 1 were waited for; matrix products, arithmetic and copies ran while one was open for 4% of the time, Pallas kernels for 0%

commit v1 on v0

v1 whole, which is shorter than its diff:
```python
import functools

import jax
import jax.numpy as jnp
from jax import lax
from jax.experimental import pallas as pl
from jax.experimental.pallas import tpu as pltpu
from jax.sharding import PartitionSpec as P

MESH = pl.DeviceIdType.MESH
LANES = 128


def layout(columns, n_op):
    width = columns // n_op
    plan, most = [], 0
    for q in range(n_op):
        pieces = []
        for tile in range(columns // LANES):
            lo, hi = max(q * width, tile * LANES), min((q + 1) * width, (tile + 1) * LANES)
            if lo < hi:
                pieces.append((tile, lo - tile * LANES, hi - tile * LANES))
        placed, at = {}, 0
        for piece in sorted(pieces, key=lambda p: p[1] - p[2]):
            rows = 32 if piece[2] - piece[1] == 64 else 64
            placed[piece] = (at, rows)
            at += rows
        plan.append([p + placed[p] for p in pieces])
        most = max(most, at)
    return plan, most


def pack(block, lo, hi):
    part = block[:, lo:hi]
    if hi - lo == LANES:
        return part
    if hi - lo == 64:
        return jnp.concatenate([part[:32], part[32:]], axis=1)
    return jnp.concatenate([part, jnp.zeros((part.shape[0], LANES - hi + lo), part.dtype)], axis=1)


def unpack(rows, width):
    if width == LANES:
        return rows
    if width == 64:
        return jnp.concatenate([rows[:, :64], rows[:, 64:]], axis=0)
    return rows[:, :width]


def kernel(n_sector, n_op, wave, left, right, delta, active, live, out,
           lhs, held, keep, up, down, below, above, zsend, zrecv,
           load_sem, up_send, up_recv, down_send, down_recv, z_send, z_recv):
    s, me = lax.axis_index("sector"), lax.axis_index("op")
    ops, rows, _ = left.shape
    columns = wave.shape[1]
    tiles = columns // LANES
    chunks = tiles // 2
    plan, most = layout(columns, n_op)

    loads = []
    for c in range(chunks):
        pair = []
        for half, tile in enumerate((c, tiles - 1 - c)):
            load = pltpu.make_async_copy(
                right.at[:, tile * LANES:(tile + 1) * LANES],
                held.at[c, :, half * LANES:(half + 1) * LANES],
                load_sem.at[c, half])
            load.start()
            pair.append(load)
        loads.append(pair)

    barrier = pltpu.get_barrier_semaphore()

    @pl.when(s > 0)
    def _():
        pl.semaphore_signal(barrier, inc=1, device_id={"sector": s - 1}, device_id_type=MESH)

    @pl.when(s < n_sector - 1)
    def _():
        pl.semaphore_signal(barrier, inc=1, device_id={"sector": s + 1}, device_id_type=MESH)

    for hop in range(1, n_op):
        pl.semaphore_signal(barrier, inc=1, device_id={"op": lax.rem(me + hop, n_op)}, device_id_type=MESH)

    on_rows = lax.broadcasted_iota(jnp.int32, (rows, columns), 0) < live[0]
    masked = jnp.where(on_rows, wave[...].astype(jnp.float32), 0.0).astype(jnp.bfloat16)
    for k in range(ops):
        inter = jnp.dot(left[k], masked, preferred_element_type=jnp.float32)
        weight = active[k].astype(jnp.float32)
        for slot, change in enumerate((0, 1, -1)):
            picked = jnp.where(delta[k] == change, weight, 0.0)
            lhs[slot * rows:(slot + 1) * rows, k * columns:(k + 1) * columns] = (inter * picked).astype(jnp.bfloat16)

    @pl.when(s == 0)
    def _():
        below[...] = jnp.zeros_like(below)

    @pl.when(s == n_sector - 1)
    def _():
        above[...] = jnp.zeros_like(above)

    near = jnp.minimum(s, 1) + jnp.minimum(n_sector - 1 - s, 1)
    pl.semaphore_wait(barrier, n_op - 1 + near)

    def to_next(c):
        return pltpu.make_async_remote_copy(
            src_ref=up.at[c], dst_ref=below.at[c], send_sem=up_send.at[c], recv_sem=up_recv.at[c],
            device_id={"sector": s + 1}, device_id_type=MESH)

    def to_previous(c):
        return pltpu.make_async_remote_copy(
            src_ref=down.at[c], dst_ref=above.at[c], send_sem=down_send.at[c], recv_sem=down_recv.at[c],
            device_id={"sector": s - 1}, device_id_type=MESH)

    def to_shard(q, index):
        _, _, _, at, size = plan[q][index]
        slot = lax.rem(me - q + n_op, n_op) - 1
        return pltpu.make_async_remote_copy(
            src_ref=zsend.at[q, at:at + size], dst_ref=zrecv.at[slot, at:at + size],
            send_sem=z_send.at[q, index], recv_sem=z_recv.at[slot, index],
            device_id={"op": q}, device_id_type=MESH)

    def from_shard(q, index, slot):
        _, _, _, at, size = plan[q][index]
        return pltpu.make_async_remote_copy(
            src_ref=zsend.at[q, at:at + size], dst_ref=zrecv.at[slot, at:at + size],
            send_sem=z_send.at[q, index], recv_sem=z_recv.at[slot, index],
            device_id={"op": lax.rem(me + slot + 1, n_op)}, device_id_type=MESH)

    def compute(c):
        for load in loads[c]:
            load.wait()
        part = jnp.dot(lhs[...], held[c], preferred_element_type=jnp.float32)
        keep[c] = part[:rows]
        up[c] = part[rows:2 * rows]
        down[c] = part[2 * rows:]

        @pl.when(s < n_sector - 1)
        def _():
            to_next(c).start()

        @pl.when(s > 0)
        def _():
            to_previous(c).start()

    def combine(c):
        @pl.when(s > 0)
        def _():
            to_next(c).wait_recv()

        @pl.when(s < n_sector - 1)
        def _():
            to_previous(c).wait_recv()

        total = keep[c] + below[c] + above[c]
        for q in range(n_op):
            for index, (tile, lo, hi, at, size) in enumerate(plan[q]):
                if tile not in (c, tiles - 1 - c):
                    continue
                half = 0 if tile == c else 1
                zsend[q, at:at + size] = pack(total[:, half * LANES:(half + 1) * LANES], lo, hi)

                @pl.when(me != q)
                def _():
                    to_shard(q, index).start()

    for c in range(chunks):
        compute(c)
        if c > 0:
            combine(c - 1)
    combine(chunks - 1)

    for q in range(n_op):
        @pl.when(me == q)
        def _():
            for slot in range(n_op - 1):
                for index in range(len(plan[q])):
                    from_shard(q, index, slot).wait_recv()
            blocks = []
            for tile, lo, hi, at, size in plan[q]:
                whole = zsend[q, at:at + size]
                for slot in range(n_op - 1):
                    whole = whole + zrecv[slot, at:at + size]
                blocks.append(unpack(whole, hi - lo))
            block = blocks[0] if len(blocks) == 1 else jnp.concatenate(blocks, axis=1)
            shown = lax.broadcasted_iota(jnp.int32, block.shape, 0) < live[0]
            out[...] = jnp.where(shown, block, 0.0).astype(out.dtype)

        @pl.when(me != q)
        def _():
            for index in range(len(plan[q])):
                to_shard(q, index).wait_send()

    @pl.when(s < n_sector - 1)
    def _():
        for c in range(chunks):
            to_next(c).wait_send()

    @pl.when(s > 0)
    def _():
        for c in range(chunks):
            to_previous(c).wait_send()


def on_device(n_sector, n_op, wave, left_blocks, right_ops, delta, active, sector_rows):
    rows, columns = wave.shape
    ops = right_ops.shape[0]
    chunks = columns // (2 * LANES)
    plan, most = layout(columns, n_op)
    pieces = max(len(p) for p in plan)
    piece = pltpu.VMEM((chunks, rows, 2 * LANES), jnp.float32)
    vmem, smem = pl.BlockSpec(memory_space=pltpu.VMEM), pl.BlockSpec(memory_space=pltpu.SMEM)
    dma = pltpu.SemaphoreType.DMA
    return pl.pallas_call(
        functools.partial(kernel, n_sector, n_op),
        out_shape=jax.ShapeDtypeStruct((rows, columns // n_op), jnp.bfloat16),
        in_specs=[vmem, vmem, pl.BlockSpec(memory_space=pl.ANY), smem, smem, smem],
        out_specs=vmem,
        scratch_shapes=[
            pltpu.VMEM((3 * rows, ops * columns), jnp.bfloat16),
            pltpu.VMEM((chunks, ops * columns, 2 * LANES), jnp.bfloat16),
            piece, piece, piece, piece, piece,
            pltpu.VMEM((n_op, most, LANES), jnp.float32),
            pltpu.VMEM((n_op - 1, most, LANES), jnp.float32),
            dma((chunks, 2)),
            dma((chunks,)), dma((chunks,)), dma((chunks,)), dma((chunks,)),
            dma((n_op, pieces)), dma((n_op - 1, pieces)),
        ],
        compiler_params=pltpu.CompilerParams(
            collective_id=0, has_side_effects=True, vmem_limit_bytes=60 * 1024 * 1024),
        name="sigma_step",
    )(wave, left_blocks, right_ops.reshape(ops * columns, columns), delta, active.reshape(ops), sector_rows)


def solution(mesh):
    return jax.shard_map(
        functools.partial(on_device, mesh.shape["sector"], mesh.shape["op"]),
        mesh=mesh,
        in_specs=(
            P("sector", None),
            P("op", "sector", None),
            P("op", None, None),
            P("op"),
            P("op", "sector"),
            P("sector"),
        ),
        out_specs=P("sector", "op"),
        check_vma=False,
    )
```

time: 130 us -> 19.6 us (0.15)
  the two profiles are of different devices: /device:TPU:1 before, /device:TPU:20 now
where the time goes in v1:
time: 19.6 us; the launch traced here: 19.4 us
  Pallas kernels  17.3 us (88%)
  local copies, waits for them, and re-layouts  1.38 us (7%)
  between operations  0.66 us (3%)
    pallas_call x1, Pallas kernels, on_device(): pl.pallas_call(functools.partial(kernel, n_sector, n_op), out_shape=jax.S...  17.3 us
    unnamed x1, local copies, waits for them, and re-layouts  1.38 us

profile of v1, /device:TPU:20, one launch (start us, length us, event | category | flops | bytes accessed | tf_op | source)
XLA Modules:
  0.0 19.4 jit_solution(17111531014769075077)
XLA Ops:
  0.7 17.3 %sigma_step.1 = bf16[64,192]{1,0:T(8,128)(2,1)} custom-call(bf16[64,768]{1,0:T(8,128)(2,1)} %wave.1, bf16[6,64,64]{2,1,0:T(8,128)(2,1)} %left.1, bf16[4608,768]{1,0:T(8,128)(2,1)} %bitcast.2, s32[6]{0:T(128)} %delta.1, s32[6]{0:T(128)} %bitcast.3, s32[1]{0:T(128)S(6)} %copy.8.live), custom_call_target="tpu_custom_call" | custom-call | tf_op jit(solution)/shard_map/sigma_step/pallas_call | solution.py:214
  18.0 1.4 %copy.9 = bf16[64,192]{1,0:T(8,128)(2,1)} copy(bf16[64,192]{1,0:T(8,128)(2,1)} %sigma_step.1) | data formatting | bytes 49152

commit v2 on v1

v2 whole, which is shorter than its diff:
```python
import functools

import jax
import jax.numpy as jnp
from jax import lax
from jax.experimental import pallas as pl
from jax.experimental.pallas import tpu as pltpu
from jax.sharding import PartitionSpec as P

MESH = pl.DeviceIdType.MESH
LANES = 128


def layout(columns, n_op):
    width = columns // n_op
    plan, most = [], 0
    for q in range(n_op):
        pieces = []
        for tile in range(columns // LANES):
            lo, hi = max(q * width, tile * LANES), min((q + 1) * width, (tile + 1) * LANES)
            if lo < hi:
                pieces.append((tile, lo - tile * LANES, hi - tile * LANES))
        placed, at = {}, 0
        for piece in sorted(pieces, key=lambda p: p[1] - p[2]):
            rows = 32 if piece[2] - piece[1] == 64 else 64
            placed[piece] = (at, rows)
            at += rows
        plan.append([p + placed[p] for p in pieces])
        most = max(most, at)
    return plan, most


def pack(block, lo, hi):
    part = block[:, lo:hi]
    if hi - lo == LANES:
        return part
    if hi - lo == 64:
        return jnp.concatenate([part[:32], part[32:]], axis=1)
    return jnp.concatenate([part, jnp.zeros((part.shape[0], LANES - hi + lo), part.dtype)], axis=1)


def unpack(rows, width):
    if width == LANES:
        return rows
    if width == 64:
        return jnp.concatenate([rows[:, :64], rows[:, 64:]], axis=0)
    return rows[:, :width]


def kernel(n_sector, n_op, wave_hbm, left_hbm, right, delta_hbm, active_hbm, live_hbm, out,
           wave, left, delta, active, live, inter, held, keep, up, down, below, above, zsend, zrecv,
           load_sem, small_sem, up_send, up_recv, down_send, down_recv, z_send, z_recv):
    s, me = lax.axis_index("sector"), lax.axis_index("op")
    ops, rows, _ = left.shape
    columns = wave.shape[1]
    tiles = columns // LANES
    chunks = tiles // 2
    plan, most = layout(columns, n_op)
    order = [tile for c in range(chunks) for tile in (c, tiles - 1 - c)]

    barrier = pltpu.get_barrier_semaphore()

    @pl.when(s > 0)
    def _():
        pl.semaphore_signal(barrier, inc=1, device_id={"sector": s - 1}, device_id_type=MESH)

    @pl.when(s < n_sector - 1)
    def _():
        pl.semaphore_signal(barrier, inc=1, device_id={"sector": s + 1}, device_id_type=MESH)

    for hop in range(1, n_op):
        pl.semaphore_signal(barrier, inc=1, device_id={"op": lax.rem(me + hop, n_op)}, device_id_type=MESH)

    small = []
    for i, (src, dst) in enumerate(((wave_hbm, wave), (left_hbm, left), (delta_hbm, delta),
                                    (active_hbm, active), (live_hbm, live))):
        small.append(pltpu.make_async_copy(src, dst, small_sem.at[i]))
        small[-1].start()

    loads = {}
    for c in range(chunks):
        for k in range(ops):
            pair = []
            for half in range(2):
                tile = order[2 * c + half]
                load = pltpu.make_async_copy(
                    right.at[k, :, tile * LANES:(tile + 1) * LANES],
                    held.at[c, k, :, half * LANES:(half + 1) * LANES],
                    load_sem.at[c, k, half])
                load.start()
                pair.append(load)
            loads[c, k] = pair

    @pl.when(s == 0)
    def _():
        below[...] = jnp.zeros_like(below)

    @pl.when(s == n_sector - 1)
    def _():
        above[...] = jnp.zeros_like(above)

    for load in small:
        load.wait()
    on_rows = lax.broadcasted_iota(jnp.int32, (rows, columns), 0) < live[0]
    masked = jnp.where(on_rows, wave[...].astype(jnp.float32), 0.0).astype(jnp.bfloat16)
    for k in range(ops):
        inter[k] = jnp.dot(left[k], masked, preferred_element_type=jnp.float32).astype(jnp.bfloat16)
    weights = [[jnp.where(delta[k] == change, active[k], 0).astype(jnp.float32) for k in range(ops)]
               for change in (0, 1, -1)]

    def to_next(i):
        return pltpu.make_async_remote_copy(
            src_ref=up.at[i], dst_ref=below.at[i], send_sem=up_send.at[i], recv_sem=up_recv.at[i],
            device_id={"sector": s + 1}, device_id_type=MESH)

    def to_previous(i):
        return pltpu.make_async_remote_copy(
            src_ref=down.at[i], dst_ref=above.at[i], send_sem=down_send.at[i], recv_sem=down_recv.at[i],
            device_id={"sector": s - 1}, device_id_type=MESH)

    def to_shard(q, index):
        _, _, _, at, size = plan[q][index]
        slot = lax.rem(me - q + n_op, n_op) - 1
        return pltpu.make_async_remote_copy(
            src_ref=zsend.at[q, at:at + size], dst_ref=zrecv.at[slot, at:at + size],
            send_sem=z_send.at[q, index], recv_sem=z_recv.at[slot, index],
            device_id={"op": q}, device_id_type=MESH)

    def from_shard(q, index, slot):
        _, _, _, at, size = plan[q][index]
        return pltpu.make_async_remote_copy(
            src_ref=zsend.at[q, at:at + size], dst_ref=zrecv.at[slot, at:at + size],
            send_sem=z_send.at[q, index], recv_sem=z_recv.at[slot, index],
            device_id={"op": lax.rem(me + slot + 1, n_op)}, device_id_type=MESH)

    def compute(c):
        sums = [None] * 3
        for k in range(ops):
            for load in loads[c, k]:
                load.wait()
            term = jnp.dot(inter[k], held[c, k], preferred_element_type=jnp.float32)
            for d in range(3):
                scaled = term * weights[d][k]
                sums[d] = scaled if k == 0 else sums[d] + scaled
        for half in range(2):
            at = slice(half * LANES, (half + 1) * LANES)
            i = 2 * c + half
            up[i] = sums[1][:, at]
            down[i] = sums[2][:, at]
            keep[i] = sums[0][:, at]

        if c == 0:
            near = jnp.minimum(s, 1) + jnp.minimum(n_sector - 1 - s, 1)
            pl.semaphore_wait(barrier, n_op - 1 + near)

        @pl.when(s < n_sector - 1)
        def _():
            for i in (2 * c, 2 * c + 1):
                to_next(i).start()

        @pl.when(s > 0)
        def _():
            for i in (2 * c, 2 * c + 1):
                to_previous(i).start()

    def combine(i):
        @pl.when(s > 0)
        def _():
            to_next(i).wait_recv()

        @pl.when(s < n_sector - 1)
        def _():
            to_previous(i).wait_recv()

        total = keep[i] + below[i] + above[i]
        for q in range(n_op):
            for index, (tile, lo, hi, at, size) in enumerate(plan[q]):
                if tile != order[i]:
                    continue
                zsend[q, at:at + size] = pack(total, lo, hi)

                @pl.when(me != q)
                def _():
                    to_shard(q, index).start()

    for c in range(chunks):
        compute(c)
    for i in range(tiles):
        combine(i)

    for q in range(n_op):
        @pl.when(me == q)
        def _():
            for slot in range(n_op - 1):
                for index in range(len(plan[q])):
                    from_shard(q, index, slot).wait_recv()
            blocks = []
            for tile, lo, hi, at, size in plan[q]:
                whole = zsend[q, at:at + size]
                for slot in range(n_op - 1):
                    whole = whole + zrecv[slot, at:at + size]
                blocks.append(unpack(whole, hi - lo))
            block = blocks[0] if len(blocks) == 1 else jnp.concatenate(blocks, axis=1)
            shown = lax.broadcasted_iota(jnp.int32, block.shape, 0) < live[0]
            out[...] = jnp.where(shown, block, 0.0)

        @pl.when(me != q)
        def _():
            for index in range(len(plan[q])):
                to_shard(q, index).wait_send()

    @pl.when(s < n_sector - 1)
    def _():
        for i in range(tiles):
            to_next(i).wait_send()

    @pl.when(s > 0)
    def _():
        for i in range(tiles):
            to_previous(i).wait_send()


def on_device(n_sector, n_op, wave, left_blocks, right_ops, delta, active, sector_rows):
    rows, columns = wave.shape
    ops = right_ops.shape[0]
    tiles = columns // LANES
    chunks = tiles // 2
    plan, most = layout(columns, n_op)
    pieces = max(len(p) for p in plan)
    piece = pltpu.VMEM((tiles, rows, LANES), jnp.float32)
    dma = pltpu.SemaphoreType.DMA
    block = pl.pallas_call(
        functools.partial(kernel, n_sector, n_op),
        out_shape=pltpu.VMEM((rows, columns // n_op), jnp.float32),
        in_specs=[pl.BlockSpec(memory_space=pltpu.HBM)] * 6,
        out_specs=pl.BlockSpec(memory_space=pltpu.VMEM),
        scratch_shapes=[
            pltpu.VMEM(wave.shape, wave.dtype),
            pltpu.VMEM(left_blocks.shape, left_blocks.dtype),
            pltpu.SMEM((ops,), jnp.int32),
            pltpu.SMEM((ops,), jnp.int32),
            pltpu.SMEM((1,), jnp.int32),
            pltpu.VMEM((ops, rows, columns), jnp.bfloat16),
            pltpu.VMEM((chunks, ops, columns, 2 * LANES), jnp.bfloat16),
            piece, piece, piece, piece, piece,
            pltpu.VMEM((n_op, most, LANES), jnp.float32),
            pltpu.VMEM((n_op - 1, most, LANES), jnp.float32),
            dma((chunks, ops, 2)), dma((5,)),
            dma((tiles,)), dma((tiles,)), dma((tiles,)), dma((tiles,)),
            dma((n_op, pieces)), dma((n_op - 1, pieces)),
        ],
        compiler_params=pltpu.CompilerParams(
            collective_id=0, has_side_effects=True, vmem_limit_bytes=60 * 1024 * 1024),
        name="sigma_step",
    )(wave, left_blocks, right_ops, delta, active.reshape(ops), sector_rows)
    return block.astype(jnp.bfloat16)


def solution(mesh):
    return jax.shard_map(
        functools.partial(on_device, mesh.shape["sector"], mesh.shape["op"]),
        mesh=mesh,
        in_specs=(
            P("sector", None),
            P("op", "sector", None),
            P("op", None, None),
            P("op"),
            P("op", "sector"),
            P("sector"),
        ),
        out_specs=P("sector", "op"),
        check_vma=False,
    )
```

time: 19.6 us -> 18.1 us (0.923)
  the two profiles are of different devices: /device:TPU:20 before, /device:TPU:1 now
where the time goes in v2:
time: 18.1 us; the launch traced here: 18 us
  Pallas kernels  16.7 us (92%)
  between operations  0.66 us (4%)
  other arithmetic  0.62 us (3%)
    pallas_call x1, Pallas kernels, on_device(): pl.pallas_call(functools.partial(kernel, n_sector, n_op), out_shape=pltpu...  16.7 us
    convert_element_type x1, other arithmetic, on_device(): return block.astype(jnp.bfloat16)  0.62 us

profile of v2, /device:TPU:1, one launch (start us, length us, event | category | flops | bytes accessed | tf_op | source)
XLA Modules:
  0.0 18.0 jit_solution(7155576834138924284)
XLA Ops:
  0.7 16.7 %sigma_step.1 = f32[64,192]{1,0:T(8,128)S(1)} custom-call(bf16[64,768]{1,0:T(8,128)(2,1)} %wave_hbm.1, bf16[6,64,64]{2,1,0:T(8,128)(2,1)} %left_hbm.1, bf16[6,768,768]{2,1,0:T(8,128)(2,1)} %right.1, s32[6]{0:T(128)} %delta_hbm.1, s32[6]{0:T(128)} %bitcast.1, s32[1]{0:T(128)S(6)} %copy.7.live_hbm), custom_call_target="tpu_custom_call" | custom-call | tf_op jit(solution)/shard_map/sigma_step/pallas_call | solution.py:232
  17.3 0.6 %convert_element_type.3 = bf16[64,192]{1,0:T(8,128)(2,1)} convert(f32[64,192]{1,0:T(8,128)S(1)} %sigma_step.1) | non-fusion elementwise | flops 12288 | bytes 73728 | tf_op jit(solution)/shard_map/convert_element_type | solution.py:256

commit v3 on v2

--- a/solution.py
+++ b/solution.py
@@ -77,19 +77,18 @@
         small.append(pltpu.make_async_copy(src, dst, small_sem.at[i]))
         small[-1].start()
 
+    groups = ((0, ops // 2), (ops // 2, ops))
     loads = {}
     for c in range(chunks):
-        for k in range(ops):
-            pair = []
+        for g, (first, last) in enumerate(groups):
             for half in range(2):
                 tile = order[2 * c + half]
                 load = pltpu.make_async_copy(
-                    right.at[k, :, tile * LANES:(tile + 1) * LANES],
-                    held.at[c, k, :, half * LANES:(half + 1) * LANES],
-                    load_sem.at[c, k, half])
+                    right.at[first:last, :, tile * LANES:(tile + 1) * LANES],
+                    held.at[c, first:last, :, half * LANES:(half + 1) * LANES],
+                    load_sem.at[c, g, half])
                 load.start()
-                pair.append(load)
-            loads[c, k] = pair
+                loads.setdefault((c, first), []).append(load)
 
     @pl.when(s == 0)
     def _():
@@ -103,8 +102,8 @@
         load.wait()
     on_rows = lax.broadcasted_iota(jnp.int32, (rows, columns), 0) < live[0]
     masked = jnp.where(on_rows, wave[...].astype(jnp.float32), 0.0).astype(jnp.bfloat16)
-    for k in range(ops):
-        inter[k] = jnp.dot(left[k], masked, preferred_element_type=jnp.float32).astype(jnp.bfloat16)
+    stacked = left[...].reshape(ops * rows, rows)
+    inter[...] = jnp.dot(stacked, masked, preferred_element_type=jnp.float32).astype(jnp.bfloat16)
     weights = [[jnp.where(delta[k] == change, active[k], 0).astype(jnp.float32) for k in range(ops)]
                for change in (0, 1, -1)]
 
@@ -136,9 +135,9 @@
     def compute(c):
         sums = [None] * 3
         for k in range(ops):
-            for load in loads[c, k]:
+            for load in loads.get((c, k), ()):
                 load.wait()
-            term = jnp.dot(inter[k], held[c, k], preferred_element_type=jnp.float32)
+            term = jnp.dot(inter[k * rows:(k + 1) * rows], held[c, k], preferred_element_type=jnp.float32)
             for d in range(3):
                 scaled = term * weights[d][k]
                 sums[d] = scaled if k == 0 else sums[d] + scaled
@@ -240,12 +239,12 @@
             pltpu.SMEM((ops,), jnp.int32),
             pltpu.SMEM((ops,), jnp.int32),
             pltpu.SMEM((1,), jnp.int32),
-            pltpu.VMEM((ops, rows, columns), jnp.bfloat16),
+            pltpu.VMEM((ops * rows, columns), jnp.bfloat16),
             pltpu.VMEM((chunks, ops, columns, 2 * LANES), jnp.bfloat16),
             piece, piece, piece, piece, piece,
             pltpu.VMEM((n_op, most, LANES), jnp.float32),
             pltpu.VMEM((n_op - 1, most, LANES), jnp.float32),
-            dma((chunks, ops, 2)), dma((5,)),
+            dma((chunks, 2, 2)), dma((5,)),
             dma((tiles,)), dma((tiles,)), dma((tiles,)), dma((tiles,)),
             dma((n_op, pieces)), dma((n_op - 1, pieces)),
         ],

time: 18.1 us -> 16.5 us (0.912)
  Pallas kernels: 16.7 us -> 15.1 us
    pallas_call x1, Pallas kernels: 16.7 us -> 15.1 us  [on_device(): pl.pallas_call(functools.partial(kernel, n_sector, n_op), out_shape=pltpu...]
where the time goes in v3:
time: 16.5 us; the launch traced here: 16.3 us
  Pallas kernels  15.1 us (92%)
  between operations  0.66 us (4%)
  other arithmetic  0.62 us (4%)
    pallas_call x1, Pallas kernels, on_device(): pl.pallas_call(functools.partial(kernel, n_sector, n_op), out_shape=pltpu...  15.1 us
    convert_element_type x1, other arithmetic, on_device(): return block.astype(jnp.bfloat16)  0.62 us

profile of v3, /device:TPU:1, one launch (start us, length us, event | category | flops | bytes accessed | tf_op | source)
XLA Modules:
  0.0 16.3 jit_solution(6947975320063771170)
XLA Ops:
  0.7 15.1 %sigma_step.1 = f32[64,192]{1,0:T(8,128)S(1)} custom-call(bf16[64,768]{1,0:T(8,128)(2,1)} %wave_hbm.1, bf16[6,64,64]{2,1,0:T(8,128)(2,1)} %left_hbm.1, bf16[6,768,768]{2,1,0:T(8,128)(2,1)} %right.1, s32[6]{0:T(128)} %delta_hbm.1, s32[6]{0:T(128)} %bitcast.1, s32[1]{0:T(128)S(6)} %copy.7.live_hbm), custom_call_target="tpu_custom_call" | custom-call | tf_op jit(solution)/shard_map/sigma_step/pallas_call | solution.py:231
  15.7 0.6 %convert_element_type.3 = bf16[64,192]{1,0:T(8,128)(2,1)} convert(f32[64,192]{1,0:T(8,128)S(1)} %sigma_step.1) | non-fusion elementwise | flops 12288 | bytes 73728 | tf_op jit(solution)/shard_map/convert_element_type | solution.py:255

commit v4 on v3

--- a/solution.py
+++ b/solution.py
@@ -77,9 +77,9 @@
         small.append(pltpu.make_async_copy(src, dst, small_sem.at[i]))
         small[-1].start()
 
-    groups = ((0, ops // 2), (ops // 2, ops))
     loads = {}
     for c in range(chunks):
+        groups = ((0, ops // 2), (ops // 2, ops)) if c == 0 else ((0, ops),)
         for g, (first, last) in enumerate(groups):
             for half in range(2):
                 tile = order[2 * c + half]

time: 16.5 us -> 15.4 us (0.933)
  Pallas kernels: 15.1 us -> 14 us
    pallas_call x1, Pallas kernels: 15.1 us -> 14 us  [on_device(): pl.pallas_call(functools.partial(kernel, n_sector, n_op), out_shape=pltpu...]
where the time goes in v4:
time: 15.4 us; the launch traced here: 15.3 us
  Pallas kernels  14 us (91%)
  between operations  0.66 us (4%)
  other arithmetic  0.62 us (4%)
    pallas_call x1, Pallas kernels, on_device(): pl.pallas_call(functools.partial(kernel, n_sector, n_op), out_shape=pltpu...  14 us
    convert_element_type x1, other arithmetic, on_device(): return block.astype(jnp.bfloat16)  0.62 us

profile of v4, /device:TPU:1, one launch (start us, length us, event | category | flops | bytes accessed | tf_op | source)
XLA Modules:
  0.0 15.3 jit_solution(15584596125948631015)
XLA Ops:
  0.7 14.0 %sigma_step.1 = f32[64,192]{1,0:T(8,128)S(1)} custom-call(bf16[64,768]{1,0:T(8,128)(2,1)} %wave_hbm.1, bf16[6,64,64]{2,1,0:T(8,128)(2,1)} %left_hbm.1, bf16[6,768,768]{2,1,0:T(8,128)(2,1)} %right.1, s32[6]{0:T(128)} %delta_hbm.1, s32[6]{0:T(128)} %bitcast.1, s32[1]{0:T(128)S(6)} %copy.7.live_hbm), custom_call_target="tpu_custom_call" | custom-call | tf_op jit(solution)/shard_map/sigma_step/pallas_call | solution.py:231
  14.7 0.6 %convert_element_type.3 = bf16[64,192]{1,0:T(8,128)(2,1)} convert(f32[64,192]{1,0:T(8,128)S(1)} %sigma_step.1) | non-fusion elementwise | flops 12288 | bytes 73728 | tf_op jit(solution)/shard_map/convert_element_type | solution.py:255
